TPU v7x, 256 devices: a whole 4x4x8 slice. The times are simulated.
256 devices in a mesh: gx: 8 (over y_hi, x), gy: 32 (over y_lo, z, core).
Axes of the slice: x: 4, y: 4 (y_hi: 2, y_lo: 2; y = y_hi * 2 + y_lo), z: 8, core: 2. Of those that a mesh axis runs over, the one named last changes fastest.
Arguments:
- white_noise: float32 [2, 32, 1024, 1024], P(None, None, 'gy', 'gx'), may hold values from -6 to 6
- head_start: float32 [2, 32, 1024, 1024], P(None, None, 'gy', 'gx'), may hold values from -6 to 6
Outputs:
- log_conductivity: float32 [2, 32, 1024, 1024], P(None, None, 'gy', 'gx')
- hydraulic_head: float32 [2, 32, 1024, 1024], P(None, None, 'gy', 'gx')
All inputs are finite; a program needn't handle non-finite values.
Results may differ from a plain program's by a relative error of at most 0.0001.
Values sent between devices are 32-bit elements; how exact they have to be, the bound alone decides.
A program may use at most 64 MiB of HBM per device.

v0:
```python
import functools
import math

import jax
import jax.numpy as jnp
import ml_dtypes
import numpy as np
from jax import lax
from jax.experimental import pallas as pl
from jax.experimental.pallas import tpu as pltpu
from jax.sharding import PartitionSpec as P

F32 = jnp.float32
BF16 = jnp.bfloat16
MESH = pl.DeviceIdType.MESH
PAD = 8


def circulant(length):
    k = np.arange(length)
    q = np.minimum(k, length - k)
    w = 2.0 * math.pi * q / length
    s = 1.0 / (1.0 + (w * (length / 16.0)) ** 2)
    a = np.sqrt(s / np.mean(s))
    taps = np.real(np.fft.ifft(a))
    return taps[(k[:, None] - k[None, :]) % length]


def split_pair(matrix):
    high = matrix.astype(ml_dtypes.bfloat16)
    low = (matrix - high.astype(np.float64)).astype(ml_dtypes.bfloat16)
    return np.stack([high, low])


def split(x):
    high = x.astype(BF16)
    low = (x - high.astype(F32)).astype(BF16)
    return high, low


def dot(a, b):
    return jnp.dot(a, b, preferred_element_type=F32)


def line_of(gx, gy, i, j):
    if (gx, gy) == (8, 32):
        core, z, y_lo = j % 2, (j // 2) % 8, j // 16
        x, y_hi = i % 4, i // 4
        t = z % 4
        x_to = (x + t % 2 + 2 * core) % 4
        y_to = (y_hi + core + t // 2) % 2
        return y_lo * 2 + z // 4, y_to * 4 + x_to
    return j // gx, (j % gx + i) % gx


def body(
    gx, gy, n, nz, yb, xb,
    w_hbm, h_hbm, c_hbm, kz_hbm, lk_hbm, ho_hbm,
    w_v, c_v, kz_v, zc, r1, acat, xo, r2, bcat, yo, lk,
    hb, rb, gb, wt, ho, row_out, row_in, col_out, col_in,
    in_sem, c_sem, s1, v1, s2, v2, s3, v3, hs, hv, out_sem,
):
    i = lax.axis_index("gx")
    j = lax.axis_index("gy")
    zc_n = nz // gx
    wide = yb + 2 * PAD
    rows = zc_n * yb
    members = range(2)

    w_in = [pltpu.make_async_copy(w_hbm.at[m], w_v.at[m], in_sem.at[m]) for m in members]
    h_in = [
        pltpu.make_async_copy(
            h_hbm.at[m], hb.at[m, :, pl.ds(PAD, yb)], in_sem.at[2 + m]
        )
        for m in members
    ]
    kz_in = pltpu.make_async_copy(kz_hbm, kz_v, c_sem.at[0])
    c_in = pltpu.make_async_copy(c_hbm, c_v, c_sem.at[1])
    kz_in.start()
    w_in[0].start()
    w_in[1].start()
    h_in[0].start()
    h_in[1].start()
    c_in.start()

    barrier = pltpu.get_barrier_semaphore()

    @pl.loop(1, gx)
    def _(k):
        pl.semaphore_signal(barrier, inc=1, device_id=((i + k) % gx, j), device_id_type=MESH)

    @pl.loop(1, gy)
    def _(k):
        pl.semaphore_signal(barrier, inc=1, device_id=(i, (j + k) % gy), device_id_type=MESH)

    def filter_z(m):
        for q in range(yb // 8):
            x = w_v[m, :, 8 * q : 8 * q + 8, :].reshape(nz * 8, xb)
            high, low = split(x)
            p = dot(kz_v[0], jnp.concatenate([high, low], axis=1))
            r = p[:, :xb] + p[:, xb:] + dot(kz_v[1], high)
            zc[m, :, 8 * q : 8 * q + 8, :] = r.reshape(nz, 8, xb)
        r1[m, i] = zc[m, pl.ds(zc_n * i, zc_n)]

    def copy1(m, peer):
        return pltpu.make_async_remote_copy(
            src_ref=zc.at[m, pl.ds(zc_n * peer, zc_n)],
            dst_ref=r1.at[m, i],
            send_sem=s1.at[m],
            recv_sem=v1.at[m],
            device_id=(peer, j),
            device_id_type=MESH,
        )

    def send1(m):
        @pl.loop(1, gx)
        def _(k):
            copy1(m, (i + k) % gx).start()

    kz_in.wait()
    w_in[0].wait()
    filter_z(0)
    pl.semaphore_wait(barrier, gx + gy - 2)
    send1(0)
    w_in[1].wait()
    filter_z(1)
    send1(1)

    lane = lax.broadcasted_iota(jnp.int32, (yb, xb), 1)
    peers = (
        ((i + gx - 1) % gx, j),
        ((i + 1) % gx, j),
        (i, (j + gy - 1) % gy),
        (i, (j + 1) % gy),
    )

    def edge_copy(field, m, side):
        out, inn = (col_out, col_in) if side < 2 else (row_out, row_in)
        return pltpu.make_async_remote_copy(
            src_ref=out.at[field, m, side % 2],
            dst_ref=inn.at[field, m, side % 2],
            send_sem=hs.at[field, m, side],
            recv_sem=hv.at[field, m, side],
            device_id=peers[side],
            device_id_type=MESH,
        )

    def send_edges(field, ref, m):
        for z in range(nz):
            row_out[field, m, 0, z : z + 1, :] = ref[m, z, PAD : PAD + 1, :]
            row_out[field, m, 1, z : z + 1, :] = ref[m, z, PAD + yb - 1 : PAD + yb, :]
        edge_copy(field, m, 2).start()
        edge_copy(field, m, 3).start()

        def pack(z, carry):
            to_left, to_right = carry
            x = ref[m, z, PAD : PAD + yb, :]
            left_at = (2 * z + xb - 1) % xb
            to_left = jnp.where(lane == left_at, pltpu.roll(x, left_at, 1), to_left)
            to_right = jnp.where(lane == 2 * z, pltpu.roll(x, 2 * z + 1, 1), to_right)
            return to_left, to_right

        zero = jnp.zeros((yb, xb), F32)
        to_left, to_right = lax.fori_loop(0, nz, pack, (zero, zero), unroll=4)
        col_out[field, m, 0] = to_left
        col_out[field, m, 1] = to_right
        edge_copy(field, m, 0).start()
        edge_copy(field, m, 1).start()

    def take_edges(field, ref, m):
        for side in range(4):
            edge_copy(field, m, side).wait_recv()
        for z in range(nz):
            ref[m, z, PAD + yb : PAD + yb + 1, :] = row_in[field, m, 0, z : z + 1, :]
            ref[m, z, PAD - 1 : PAD, :] = row_in[field, m, 1, z : z + 1, :]
        return jnp.where(lane % 2 == 0, col_in[field, m, 1], col_in[field, m, 0])

    for m in members:
        h_in[m].wait()
        send_edges(0, hb, m)

    def wait_all(ref, sem):
        pltpu.make_async_copy(ref, ref, sem).wait()

    def copy2(m, k):
        jp = (j + k) % gy
        a, xe = line_of(gx, gy, i, jp)
        return pltpu.make_async_remote_copy(
            src_ref=xo.at[m, xe, pl.ds(yb * a, yb)],
            dst_ref=r2.at[m, j],
            send_sem=s2.at[m],
            recv_sem=v2.at[m],
            device_id=(i, jp),
            device_id_type=MESH,
        )

    my_a, my_xe = line_of(gx, gy, i, j)

    def filter_x(m):
        for s in range(gx):
            high, low = split(r1[m, s].reshape(rows, xb))
            acat[0:rows, s * xb : (s + 1) * xb] = high
            acat[rows : 2 * rows, s * xb : (s + 1) * xb] = low
        for c in range(n // (2 * xb)):
            cols = slice(2 * xb * c, 2 * xb * (c + 1))
            p = dot(acat[...], c_v[0, :, cols])
            r = p[:rows] + p[rows:] + dot(acat[0:rows, :], c_v[1, :, cols])
            xo[m, 2 * c] = r[:, :xb]
            xo[m, 2 * c + 1] = r[:, xb:]
        r2[m, j] = xo[m, my_xe, pl.ds(yb * my_a, yb), :]

    c_in.wait()
    for m in members:
        wait_all(r1.at[m, pl.ds(0, gx - 1)], v1.at[m])
        filter_x(m)

        @pl.loop(1, gy)
        def _(k):
            copy2(m, k).start()

    my_z = zc_n * i + my_a

    def copy3(m, jp):
        return pltpu.make_async_remote_copy(
            src_ref=yo.at[m, jp],
            dst_ref=lk.at[m, my_z],
            send_sem=s3.at[m],
            recv_sem=v3.at[m],
            device_id=(my_xe, jp),
            device_id_type=MESH,
        )

    def keep3(m):
        return pltpu.make_async_copy(yo.at[m, j], lk.at[m, my_z], v3.at[m])

    def filter_y(m):
        per = 256 // yb
        for s in range(gy):
            high, low = split(r2[m, s])
            bcat[s * yb : (s + 1) * yb, 0:xb] = high
            bcat[s * yb : (s + 1) * yb, xb : 2 * xb] = low
        for c in range(n // 256):
            lines = slice(256 * c, 256 * (c + 1))
            p = dot(c_v[0, lines, :], bcat[...])
            r = p[:, :xb] + p[:, xb:] + dot(c_v[1, lines, :], bcat[:, 0:xb])
            yo[m, per * c : per * (c + 1)] = r.reshape(per, yb, xb)

    for m in members:
        wait_all(r2.at[m, pl.ds(0, gy - 1)], v2.at[m])
        filter_y(m)

        @pl.when(my_xe != i)
        def _():
            copy3(m, j).start()

        @pl.when(my_xe == i)
        def _():
            keep3(m).start()

        @pl.loop(1, gy)
        def _(k):
            copy3(m, (j + k) % gy).start()

    row_at = yb * j + lax.broadcasted_iota(jnp.int32, (yb, xb), 0)
    col_at = xb * i + lane
    pinned = (row_at == 0) | (row_at == n - 1) | (col_at == 0) | (col_at == n - 1)

    def sides(ref, m, z, edge):
        x = ref[m, z, PAD : PAD + yb, :]
        e = pltpu.roll(edge, (xb - 2 * z) % xb, 1)
        left = jnp.where(lane == 0, e, pltpu.roll(x, 1, 1))
        right = jnp.where(lane == xb - 1, e, pltpu.roll(x, xb - 1, 1))
        up = ref[m, z, PAD - 1 : PAD - 1 + yb, :]
        down = ref[m, z, PAD + 1 : PAD + 1 + yb, :]
        below = ref[m, z - 1, PAD : PAD + yb, :]
        above = ref[m, z + 1, PAD : PAD + yb, :]
        return x, (left, right, up, down, below, above)

    for m in members:
        wait_all(lk.at[m], v3.at[m])
        pltpu.make_async_copy(lk.at[m], lk_hbm.at[m], out_sem.at[m]).start()

        @pl.loop(0, nz)
        def _(z):
            rb[m, z, PAD : PAD + yb, :] = jnp.exp(-lk[m, z])

        send_edges(1, rb, m)
        h_edge = take_edges(0, hb, m)
        r_edge = take_edges(1, rb, m)

        gb[m, 0, PAD : PAD + yb, :] = hb[m, 0, PAD : PAD + yb, :]
        gb[m, nz - 1, PAD : PAD + yb, :] = hb[m, nz - 1, PAD : PAD + yb, :]
        ho[m, 0] = hb[m, 0, PAD : PAD + yb, :]
        ho[m, nz - 1] = hb[m, nz - 1, PAD : PAD + yb, :]

        @pl.loop(1, nz - 1)
        def _(z):
            r, r_sides = sides(rb, m, z, r_edge)
            h, h_sides = sides(hb, m, z, h_edge)
            weights = [1.0 / (r + r_side) for r_side in r_sides]
            total = sum(weights[1:], weights[0])
            inverse = 1.0 / total
            new = jnp.zeros_like(h)
            for d in range(6):
                weight = weights[d] * inverse
                wt[z, d] = weight
                new = new + weight * h_sides[d]
            gb[m, z, PAD : PAD + yb, :] = jnp.where(pinned, h, new)

        send_edges(2, gb, m)
        g_edge = take_edges(2, gb, m)

        @pl.loop(1, nz - 1)
        def _(z):
            h, h_sides = sides(gb, m, z, g_edge)
            new = jnp.zeros_like(h)
            for d in range(6):
                new = new + wt[z, d] * h_sides[d]
            ho[m, z] = jnp.where(pinned, h, new)

        pltpu.make_async_copy(ho.at[m], ho_hbm.at[m], out_sem.at[2 + m]).start()

    for m in members:
        pltpu.make_async_copy(lk.at[m], lk_hbm.at[m], out_sem.at[m]).wait()
        pltpu.make_async_copy(ho.at[m], ho_hbm.at[m], out_sem.at[2 + m]).wait()
        for field in range(3):
            for side in range(4):
                edge_copy(field, m, side).wait_send()

        @pl.loop(1, gx)
        def _(k):
            copy1(m, (i + k) % gx).wait_send()

        @pl.loop(1, gy)
        def _(k):
            copy2(m, k).wait_send()

        @pl.when(my_xe != i)
        def _():
            copy3(m, j).wait_send()

        @pl.loop(1, gy)
        def _(k):
            copy3(m, (j + k) % gy).wait_send()


def on_device(gx, gy, white_noise, head_start):
    _, nz, yb, xb = white_noise.shape
    n = yb * gy
    assert n == xb * gx
    zc_n = nz // gx
    rows = zc_n * yb
    wide = yb + 2 * PAD
    matrix = jnp.asarray(split_pair(circulant(n)))
    z_matrix = jnp.asarray(split_pair(np.kron(circulant(nz), np.eye(8))))
    block = jax.ShapeDtypeStruct(white_noise.shape, F32)
    dma = pltpu.SemaphoreType.DMA
    return pl.pallas_call(
        functools.partial(body, gx, gy, n, nz, yb, xb),
        out_shape=(block, block),
        in_specs=[pl.BlockSpec(memory_space=pl.ANY)] * 4,
        out_specs=(pl.BlockSpec(memory_space=pl.ANY),) * 2,
        scratch_shapes=[
            pltpu.VMEM((2, nz, yb, xb), F32),
            pltpu.VMEM((2, n, n), BF16),
            pltpu.VMEM((2, nz * 8, nz * 8), BF16),
            pltpu.VMEM((2, nz, yb, xb), F32),
            pltpu.VMEM((2, gx, zc_n, yb, xb), F32),
            pltpu.VMEM((2 * rows, n), BF16),
            pltpu.VMEM((2, gx, rows, xb), F32),
            pltpu.VMEM((2, gy, yb, xb), F32),
            pltpu.VMEM((n, 2 * xb), BF16),
            pltpu.VMEM((2, gy, yb, xb), F32),
            pltpu.VMEM((2, nz, yb, xb), F32),
            pltpu.VMEM((2, nz, wide, xb), F32),
            pltpu.VMEM((2, nz, wide, xb), F32),
            pltpu.VMEM((2, nz, wide, xb), F32),
            pltpu.VMEM((nz, 6, yb, xb), F32),
            pltpu.VMEM((2, nz, yb, xb), F32),
            pltpu.VMEM((3, 2, 2, nz, xb), F32),
            pltpu.VMEM((3, 2, 2, nz, xb), F32),
            pltpu.VMEM((3, 2, 2, yb, xb), F32),
            pltpu.VMEM((3, 2, 2, yb, xb), F32),
            dma((4,)),
            dma((2,)),
            dma((2,)), dma((2,)),
            dma((2,)), dma((2,)),
            dma((2,)), dma((2,)),
            dma((3, 2, 4)), dma((3, 2, 4)),
            dma((4,)),
        ],
        compiler_params=pltpu.CompilerParams(
            collective_id=0, has_side_effects=True, vmem_limit_bytes=48 * 1024 * 1024
        ),
        cost_estimate=pl.CostEstimate(
            flops=6 * 2 * rows * 2 * n * n, bytes_accessed=16 * n * xb * 4, transcendentals=2 * nz * yb * xb
        ),
    )(white_noise, head_start, matrix, z_matrix)


def solution(mesh):
    spec = P(None, None, "gy", "gx")
    return jax.shard_map(
        functools.partial(on_device, mesh.shape["gx"], mesh.shape["gy"]),
        mesh=mesh,
        in_specs=(spec, spec),
        out_specs=(spec, spec),
        check_vma=False,
    )
```

profile of v0, /device:TPU:1, one launch (start us, length us, event | category | flops | bytes accessed | tf_op | source)
XLA Modules:
  0.0 101.3 jit_solution(9385445869869321592)
XLA Ops:
  0.6 0.0 copy-start
  0.6 1.2 %copy-done = f32[2,32,32,128]{3,2,1,0:T(8,128)S(1)} copy-done((f32[2,32,32,128]{3,2,1,0:T(8,128)S(1)}, f32[2,32,32,128]{3,2,1,0:T(8,128)}, u32[]{:S(2)}) %copy-start) | copy-done | bytes 1048600
  1.9 0.0 copy-start.1
  1.9 1.2 %copy-done.1 = f32[2,32,32,128]{3,2,1,0:T(8,128)S(1)} copy-done((f32[2,32,32,128]{3,2,1,0:T(8,128)S(1)}, f32[2,32,32,128]{3,2,1,0:T(8,128)}, u32[]{:S(2)}) %copy-start.1) | copy-done | bytes 1048600
  3.1 0.0 copy-start.2
  3.1 0.9 copy-done.2
  4.0 95.3 %shard_map.59 = (f32[2,32,32,128]{3,2,1,0:T(8,128)S(1)}, f32[2,32,32,128]{3,2,1,0:T(8,128)S(1)}) custom-call(f32[2,32,32,128]{3,2,1,0:T(8,128)S(1)} %copy-done, f32[2,32,32,128]{3,2,1,0:T(8,128)S(1)} %copy-done.1, bf16[2,1024,1024]{2,1,0:T(8,128)(2,1)} %constant.4.clone.c_hbm, bf16[2,256,256]{2,1,0:T(8,128)(2,1)S(1)} %copy-done.2), custom_call_target="tpu_custom_call" | custom-call | flops 3221225472 | bytes 8388608 | tf_op jit(solution)/shard_map/pallas_call | solution.py:358
  99.3 1.0 copy.8
  100.3 1.0 copy.9
Async XLA Ops:
  0.6 1.2 %copy-start = (f32[2,32,32,128]{3,2,1,0:T(8,128)S(1)}, f32[2,32,32,128]{3,2,1,0:T(8,128)}, u32[]{:S(2)}) copy-start(f32[2,32,32,128]{3,2,1,0:T(8,128)} %w_hbm.1) | copy-start | bytes 3145732
  1.9 1.2 %copy-start.1 = (f32[2,32,32,128]{3,2,1,0:T(8,128)S(1)}, f32[2,32,32,128]{3,2,1,0:T(8,128)}, u32[]{:S(2)}) copy-start(f32[2,32,32,128]{3,2,1,0:T(8,128)} %h_hbm.1) | copy-start | bytes 3145732
  3.1 0.9 copy-start.2
where the time goes:
time: 101 us
  Pallas kernels  95.3 us (94%)
  local copies, waits for them, and re-layouts  5.33 us (5%)
    pallas_call x1, Pallas kernels, on_device(): pl.pallas_call(functools.partial(body, gx, gy, n, nz, yb, xb), out_shape=...  95.3 us
    unnamed x8, local copies, waits for them, and re-layouts  5.33 us

commit v1 on v0

--- a/solution.py
+++ b/solution.py
@@ -42,29 +42,26 @@
     return jnp.dot(a, b, preferred_element_type=F32)
 
 
-def line_of(gx, gy, i, j):
+def blocks_of(gx, gy, i, j, s):
     if (gx, gy) == (8, 32):
         core, z, y_lo = j % 2, (j // 2) % 8, j // 16
         x, y_hi = i % 4, i // 4
-        t = z % 4
-        x_to = (x + t % 2 + 2 * core) % 4
-        y_to = (y_hi + core + t // 2) % 2
-        return y_lo * 2 + z // 4, y_to * 4 + x_to
-    return j // gx, (j % gx + i) % gx
+        turn = (x + 2 * core * x) % 4
+        return (y_lo + y_hi) % 2 * 16 + (z + turn + 4 * s) % 8 * 2
+    return gy // gx * i + 2 * s
 
 
 def body(
     gx, gy, n, nz, yb, xb,
     w_hbm, h_hbm, c_hbm, kz_hbm, lk_hbm, ho_hbm,
-    w_v, c_v, kz_v, zc, r1, acat, xo, r2, bcat, yo, lk,
+    w_v, c_v, kz_v, zc, r1, bcat, yo, r2, acat, xo, lk,
     hb, rb, gb, wt, ho, row_out, row_in, col_out, col_in,
     in_sem, c_sem, s1, v1, s2, v2, s3, v3, hs, hv, out_sem,
 ):
     i = lax.axis_index("gx")
     j = lax.axis_index("gy")
-    zc_n = nz // gx
     wide = yb + 2 * PAD
-    rows = zc_n * yb
+    rows = 4 * yb
     members = range(2)
 
     w_in = [pltpu.make_async_copy(w_hbm.at[m], w_v.at[m], in_sem.at[m]) for m in members]
@@ -100,22 +97,23 @@
             p = dot(kz_v[0], jnp.concatenate([high, low], axis=1))
             r = p[:, :xb] + p[:, xb:] + dot(kz_v[1], high)
             zc[m, :, 8 * q : 8 * q + 8, :] = r.reshape(nz, 8, xb)
-        r1[m, i] = zc[m, pl.ds(zc_n * i, zc_n)]
-
-    def copy1(m, peer):
+        r1[m, j] = zc[m, j]
+
+    def copy1(m, k):
+        peer = (j + k) % gy
         return pltpu.make_async_remote_copy(
-            src_ref=zc.at[m, pl.ds(zc_n * peer, zc_n)],
-            dst_ref=r1.at[m, i],
+            src_ref=zc.at[m, peer],
+            dst_ref=r1.at[m, j],
             send_sem=s1.at[m],
             recv_sem=v1.at[m],
-            device_id=(peer, j),
+            device_id=(i, peer),
             device_id_type=MESH,
         )
 
     def send1(m):
-        @pl.loop(1, gx)
+        @pl.loop(1, gy)
         def _(k):
-            copy1(m, (i + k) % gx).start()
+            copy1(m, k).start()
 
     kz_in.wait()
     w_in[0].wait()
@@ -182,61 +180,20 @@
     def wait_all(ref, sem):
         pltpu.make_async_copy(ref, ref, sem).wait()
 
-    def copy2(m, k):
-        jp = (j + k) % gy
-        a, xe = line_of(gx, gy, i, jp)
+    def copy2(m, to, s):
         return pltpu.make_async_remote_copy(
-            src_ref=xo.at[m, xe, pl.ds(yb * a, yb)],
-            dst_ref=r2.at[m, j],
+            src_ref=yo.at[m, pl.ds(blocks_of(gx, gy, to, j, s), 2)],
+            dst_ref=r2.at[m, i, s],
             send_sem=s2.at[m],
             recv_sem=v2.at[m],
-            device_id=(i, jp),
+            device_id=(to, j),
             device_id_type=MESH,
         )
-
-    my_a, my_xe = line_of(gx, gy, i, j)
-
-    def filter_x(m):
-        for s in range(gx):
-            high, low = split(r1[m, s].reshape(rows, xb))
-            acat[0:rows, s * xb : (s + 1) * xb] = high
-            acat[rows : 2 * rows, s * xb : (s + 1) * xb] = low
-        for c in range(n // (2 * xb)):
-            cols = slice(2 * xb * c, 2 * xb * (c + 1))
-            p = dot(acat[...], c_v[0, :, cols])
-            r = p[:rows] + p[rows:] + dot(acat[0:rows, :], c_v[1, :, cols])
-            xo[m, 2 * c] = r[:, :xb]
-            xo[m, 2 * c + 1] = r[:, xb:]
-        r2[m, j] = xo[m, my_xe, pl.ds(yb * my_a, yb), :]
-
-    c_in.wait()
-    for m in members:
-        wait_all(r1.at[m, pl.ds(0, gx - 1)], v1.at[m])
-        filter_x(m)
-
-        @pl.loop(1, gy)
-        def _(k):
-            copy2(m, k).start()
-
-    my_z = zc_n * i + my_a
-
-    def copy3(m, jp):
-        return pltpu.make_async_remote_copy(
-            src_ref=yo.at[m, jp],
-            dst_ref=lk.at[m, my_z],
-            send_sem=s3.at[m],
-            recv_sem=v3.at[m],
-            device_id=(my_xe, jp),
-            device_id_type=MESH,
-        )
-
-    def keep3(m):
-        return pltpu.make_async_copy(yo.at[m, j], lk.at[m, my_z], v3.at[m])
 
     def filter_y(m):
         per = 256 // yb
         for s in range(gy):
-            high, low = split(r2[m, s])
+            high, low = split(r1[m, s])
             bcat[s * yb : (s + 1) * yb, 0:xb] = high
             bcat[s * yb : (s + 1) * yb, xb : 2 * xb] = low
         for c in range(n // 256):
@@ -244,22 +201,62 @@
             p = dot(c_v[0, lines, :], bcat[...])
             r = p[:, :xb] + p[:, xb:] + dot(c_v[1, lines, :], bcat[:, 0:xb])
             yo[m, per * c : per * (c + 1)] = r.reshape(per, yb, xb)
-
+        for s in range(2):
+            r2[m, i, s] = yo[m, pl.ds(blocks_of(gx, gy, i, j, s), 2)]
+
+        @pl.loop(1, gx)
+        def _(k):
+            for s in range(2):
+                copy2(m, (i + k) % gx, s).start()
+
+    def copy3(m, to, s, c):
+        return pltpu.make_async_remote_copy(
+            src_ref=xo.at[m, to, s, c],
+            dst_ref=lk.at[m, j],
+            send_sem=s3.at[m],
+            recv_sem=v3.at[m],
+            device_id=(to, blocks_of(gx, gy, i, j, s) + c),
+            device_id_type=MESH,
+        )
+
+    def each3(m, here, there):
+        @pl.loop(0, gx)
+        def _(k):
+            to = (i + k) % gx
+            for s in range(2):
+                for c in range(2):
+                    own = (to == i) & (blocks_of(gx, gy, i, j, s) + c == j)
+
+                    @pl.when(own)
+                    def _():
+                        here(m, to, s, c)
+
+                    @pl.when(jnp.logical_not(own))
+                    def _():
+                        there(m, to, s, c)
+
+    def keep3(m, to, s, c):
+        pltpu.make_async_copy(xo.at[m, to, s, c], lk.at[m, j], v3.at[m]).start()
+
+    def filter_x(m):
+        for s in range(gx):
+            high, low = split(r2[m, s].reshape(rows, xb))
+            acat[0:rows, s * xb : (s + 1) * xb] = high
+            acat[rows : 2 * rows, s * xb : (s + 1) * xb] = low
+        for c in range(n // (2 * xb)):
+            cols = slice(2 * xb * c, 2 * xb * (c + 1))
+            p = dot(acat[...], c_v[0, :, cols])
+            r = p[:rows] + p[rows:] + dot(acat[0:rows, :], c_v[1, :, cols])
+            xo[m, 2 * c] = r[:, :xb].reshape(2, 2, yb, xb)
+            xo[m, 2 * c + 1] = r[:, xb:].reshape(2, 2, yb, xb)
+        each3(m, keep3, lambda *at: copy3(*at).start())
+
+    c_in.wait()
     for m in members:
-        wait_all(r2.at[m, pl.ds(0, gy - 1)], v2.at[m])
+        wait_all(r1.at[m, pl.ds(0, gy - 1)], v1.at[m])
         filter_y(m)
-
-        @pl.when(my_xe != i)
-        def _():
-            copy3(m, j).start()
-
-        @pl.when(my_xe == i)
-        def _():
-            keep3(m).start()
-
-        @pl.loop(1, gy)
-        def _(k):
-            copy3(m, (j + k) % gy).start()
+        wait_all(r2.at[m, pl.ds(0, gx - 1)], v2.at[m])
+        filter_x(m)
 
     row_at = yb * j + lax.broadcasted_iota(jnp.int32, (yb, xb), 0)
     col_at = xb * i + lane
@@ -327,29 +324,24 @@
             for side in range(4):
                 edge_copy(field, m, side).wait_send()
 
+        @pl.loop(1, gy)
+        def _(k):
+            copy1(m, k).wait_send()
+
         @pl.loop(1, gx)
         def _(k):
-            copy1(m, (i + k) % gx).wait_send()
-
-        @pl.loop(1, gy)
-        def _(k):
-            copy2(m, k).wait_send()
-
-        @pl.when(my_xe != i)
-        def _():
-            copy3(m, j).wait_send()
-
-        @pl.loop(1, gy)
-        def _(k):
-            copy3(m, (j + k) % gy).wait_send()
+            for s in range(2):
+                copy2(m, (i + k) % gx, s).wait_send()
+
+        each3(m, lambda *at: None, lambda *at: copy3(*at).wait_send())
 
 
 def on_device(gx, gy, white_noise, head_start):
     _, nz, yb, xb = white_noise.shape
     n = yb * gy
     assert n == xb * gx
-    zc_n = nz // gx
-    rows = zc_n * yb
+    assert n == 4 * yb * gx and nz == gy
+    rows = 4 * yb
     wide = yb + 2 * PAD
     matrix = jnp.asarray(split_pair(circulant(n)))
     z_matrix = jnp.asarray(split_pair(np.kron(circulant(nz), np.eye(8))))
@@ -365,12 +357,12 @@
             pltpu.VMEM((2, n, n), BF16),
             pltpu.VMEM((2, nz * 8, nz * 8), BF16),
             pltpu.VMEM((2, nz, yb, xb), F32),
-            pltpu.VMEM((2, gx, zc_n, yb, xb), F32),
-            pltpu.VMEM((2 * rows, n), BF16),
-            pltpu.VMEM((2, gx, rows, xb), F32),
             pltpu.VMEM((2, gy, yb, xb), F32),
             pltpu.VMEM((n, 2 * xb), BF16),
             pltpu.VMEM((2, gy, yb, xb), F32),
+            pltpu.VMEM((2, gx, 2, 2, yb, xb), F32),
+            pltpu.VMEM((2 * rows, n), BF16),
+            pltpu.VMEM((2, gx, 2, 2, yb, xb), F32),
             pltpu.VMEM((2, nz, yb, xb), F32),
             pltpu.VMEM((2, nz, wide, xb), F32),
             pltpu.VMEM((2, nz, wide, xb), F32),
@@ -390,7 +382,7 @@
             dma((4,)),
         ],
         compiler_params=pltpu.CompilerParams(
-            collective_id=0, has_side_effects=True, vmem_limit_bytes=48 * 1024 * 1024
+            collective_id=0, has_side_effects=True, vmem_limit_bytes=60 * 1024 * 1024
         ),
         cost_estimate=pl.CostEstimate(
             flops=6 * 2 * rows * 2 * n * n, bytes_accessed=16 * n * xb * 4, transcendentals=2 * nz * yb * xb

time: 101 us -> 107 us (1.059)
  the two profiles are of different devices: /device:TPU:1 before, /device:TPU:24 now
where the time goes in v1:
time: 107 us
  Pallas kernels  102 us (95%)
  local copies, waits for them, and re-layouts  4.52 us (4%)
    pallas_call x1, Pallas kernels, on_device(): pl.pallas_call(functools.partial(body, gx, gy, n, nz, yb, xb), out_shape=...  102 us
    unnamed x2, local copies, waits for them, and re-layouts  4.52 us

profile of v1, /device:TPU:24, one launch (start us, length us, event | category | flops | bytes accessed | tf_op | source)
XLA Modules:
  0.0 107.3 jit_solution(5470870088066247387)
XLA Ops:
  0.6 102.1 %shard_map.59 = (f32[2,32,32,128]{3,2,1,0:T(8,128)}, f32[2,32,32,128]{3,2,1,0:T(8,128)}) custom-call(f32[2,32,32,128]{3,2,1,0:T(8,128)} %w_hbm.1, f32[2,32,32,128]{3,2,1,0:T(8,128)} %h_hbm.1, bf16[2,1024,1024]{2,1,0:T(8,128)(2,1)} %constant.4.clone.c_hbm, bf16[2,256,256]{2,1,0:T(8,128)(2,1)} %constant.5.clone.kz_hbm), custom_call_target="tpu_custom_call" | custom-call | flops 3221225472 | bytes 8388608 | tf_op jit(solution)/shard_map/pallas_call | solution.py:350
  102.8 2.3 %copy.8 = f32[2,32,32,128]{3,2,1,0:T(8,128)} copy(f32[2,32,32,128]{3,2,1,0:T(8,128)} %get-tuple-element.4) | data formatting | bytes 2097152
  105.0 2.3 %copy.9 = f32[2,32,32,128]{3,2,1,0:T(8,128)} copy(f32[2,32,32,128]{3,2,1,0:T(8,128)} %get-tuple-element.5) | data formatting | bytes 2097152

commit v2 on v1

--- a/solution.py
+++ b/solution.py
@@ -125,6 +125,8 @@
     send1(1)
 
     lane = lax.broadcasted_iota(jnp.int32, (yb, xb), 1)
+    first, last = lane == 0, lane == xb - 1
+    even = lane % 2 == 0
     peers = (
         ((i + gx - 1) % gx, j),
         ((i + 1) % gx, j),
@@ -143,27 +145,22 @@
             device_id_type=MESH,
         )
 
-    def send_edges(field, ref, m):
-        for z in range(nz):
-            row_out[field, m, 0, z : z + 1, :] = ref[m, z, PAD : PAD + 1, :]
-            row_out[field, m, 1, z : z + 1, :] = ref[m, z, PAD + yb - 1 : PAD + yb, :]
-        edge_copy(field, m, 2).start()
-        edge_copy(field, m, 3).start()
-
-        def pack(z, carry):
-            to_left, to_right = carry
-            x = ref[m, z, PAD : PAD + yb, :]
-            left_at = (2 * z + xb - 1) % xb
-            to_left = jnp.where(lane == left_at, pltpu.roll(x, left_at, 1), to_left)
-            to_right = jnp.where(lane == 2 * z, pltpu.roll(x, 2 * z + 1, 1), to_right)
-            return to_left, to_right
-
-        zero = jnp.zeros((yb, xb), F32)
-        to_left, to_right = lax.fori_loop(0, nz, pack, (zero, zero), unroll=4)
-        col_out[field, m, 0] = to_left
-        col_out[field, m, 1] = to_right
-        edge_copy(field, m, 0).start()
-        edge_copy(field, m, 1).start()
+    zero = jnp.zeros((yb, xb), F32)
+
+    def pack(field, m, z, x, packed):
+        to_left, to_right = packed
+        row_out[field, m, 0, pl.ds(z, 1), :] = x[0:1]
+        row_out[field, m, 1, pl.ds(z, 1), :] = x[yb - 1 : yb]
+        left_at = (2 * z + xb - 1) % xb
+        to_left = jnp.where(lane == left_at, pltpu.roll(x, left_at, 1), to_left)
+        to_right = jnp.where(lane == 2 * z, pltpu.roll(x, 2 * z + 1, 1), to_right)
+        return to_left, to_right
+
+    def send_edges(field, m, packed):
+        col_out[field, m, 0] = packed[0]
+        col_out[field, m, 1] = packed[1]
+        for side in range(4):
+            edge_copy(field, m, side).start()
 
     def take_edges(field, ref, m):
         for side in range(4):
@@ -171,11 +168,20 @@
         for z in range(nz):
             ref[m, z, PAD + yb : PAD + yb + 1, :] = row_in[field, m, 0, z : z + 1, :]
             ref[m, z, PAD - 1 : PAD, :] = row_in[field, m, 1, z : z + 1, :]
-        return jnp.where(lane % 2 == 0, col_in[field, m, 1], col_in[field, m, 0])
+        return jnp.where(even, col_in[field, m, 1], col_in[field, m, 0])
+
+    def own_edges(field, m):
+        left = pltpu.roll(col_out[field, m, 0], 1, 1)
+        right = pltpu.roll(col_out[field, m, 1], xb - 1, 1)
+        return jnp.where(even, left, right)
 
     for m in members:
         h_in[m].wait()
-        send_edges(0, hb, m)
+
+        def pack_head(z, packed):
+            return pack(0, m, z, hb[m, z, PAD : PAD + yb, :], packed)
+
+        send_edges(0, m, lax.fori_loop(0, nz, pack_head, (zero, zero), unroll=16))
 
     def wait_all(ref, sem):
         pltpu.make_async_copy(ref, ref, sem).wait()
@@ -262,59 +268,89 @@
     col_at = xb * i + lane
     pinned = (row_at == 0) | (row_at == n - 1) | (col_at == 0) | (col_at == n - 1)
 
-    def sides(ref, m, z, edge):
-        x = ref[m, z, PAD : PAD + yb, :]
-        e = pltpu.roll(edge, (xb - 2 * z) % xb, 1)
-        left = jnp.where(lane == 0, e, pltpu.roll(x, 1, 1))
-        right = jnp.where(lane == xb - 1, e, pltpu.roll(x, xb - 1, 1))
-        up = ref[m, z, PAD - 1 : PAD - 1 + yb, :]
-        down = ref[m, z, PAD + 1 : PAD + 1 + yb, :]
-        below = ref[m, z - 1, PAD : PAD + yb, :]
-        above = ref[m, z + 1, PAD : PAD + yb, :]
-        return x, (left, right, up, down, below, above)
+    def inverse(x):
+        guess = pl.reciprocal(x, approx=True)
+        return guess * (2.0 - x * guess)
+
+    def layer(ref, m, z):
+        return ref[m, z, PAD : PAD + yb, :]
+
+    def above(ref, m, z):
+        return ref[m, z, PAD - 1 : PAD - 1 + yb, :]
+
+    def under(ref, m, z):
+        return ref[m, z, PAD + 1 : PAD + 1 + yb, :]
+
+    def to_lane(packed, z):
+        return pltpu.roll(packed, (xb - 2 * z) % xb, 1)
+
+    def flow_x(w, h, edge_w, edge_h, z):
+        right = jnp.where(last, to_lane(edge_w, z), w)
+        w_left = jnp.where(first, to_lane(edge_w, z), pltpu.roll(w, 1, 1))
+        e = to_lane(edge_h, z)
+        h_right = jnp.where(last, e, pltpu.roll(h, xb - 1, 1))
+        h_left = jnp.where(first, e, pltpu.roll(h, 1, 1))
+        return right * h_right + w_left * h_left, right + w_left
 
     for m in members:
         wait_all(lk.at[m], v3.at[m])
         pltpu.make_async_copy(lk.at[m], lk_hbm.at[m], out_sem.at[m]).start()
 
-        @pl.loop(0, nz)
-        def _(z):
-            rb[m, z, PAD : PAD + yb, :] = jnp.exp(-lk[m, z])
-
-        send_edges(1, rb, m)
+        def resist(z, packed):
+            r = jnp.exp(-lk[m, z])
+            rb[m, z, PAD : PAD + yb, :] = r
+            return pack(1, m, z, r, packed)
+
+        send_edges(1, m, lax.fori_loop(0, nz, resist, (zero, zero), unroll=True))
         h_edge = take_edges(0, hb, m)
         r_edge = take_edges(1, rb, m)
-
-        gb[m, 0, PAD : PAD + yb, :] = hb[m, 0, PAD : PAD + yb, :]
-        gb[m, nz - 1, PAD : PAD + yb, :] = hb[m, nz - 1, PAD : PAD + yb, :]
-        ho[m, 0] = hb[m, 0, PAD : PAD + yb, :]
-        ho[m, nz - 1] = hb[m, nz - 1, PAD : PAD + yb, :]
-
-        @pl.loop(1, nz - 1)
-        def _(z):
-            r, r_sides = sides(rb, m, z, r_edge)
-            h, h_sides = sides(hb, m, z, h_edge)
-            weights = [1.0 / (r + r_side) for r_side in r_sides]
-            total = sum(weights[1:], weights[0])
-            inverse = 1.0 / total
-            new = jnp.zeros_like(h)
-            for d in range(6):
-                weight = weights[d] * inverse
-                wt[z, d] = weight
-                new = new + weight * h_sides[d]
-            gb[m, z, PAD : PAD + yb, :] = jnp.where(pinned, h, new)
-
-        send_edges(2, gb, m)
+        w_edge = inverse(own_edges(1, m) + r_edge)
+
+        for z in (0, nz - 1):
+            gb[m, z, PAD : PAD + yb, :] = layer(hb, m, z)
+            ho[m, z] = layer(hb, m, z)
+
+        def sweep(z, carry):
+            r, h_low, h, w_low, packed = carry
+            r_high = layer(rb, m, z + 1)
+            h_high = layer(hb, m, z + 1)
+            w_high = inverse(r + r_high)
+            w_up = inverse(r + above(rb, m, z))
+            w_down = inverse(r + under(rb, m, z))
+            w_x = inverse(r + pltpu.roll(r, xb - 1, 1))
+            gain, total = flow_x(w_x, h, w_edge, h_edge, z)
+            total = total + ((w_low + w_high) + (w_up + w_down))
+            gain = gain + (w_low * h_low + w_high * h_high)
+            gain = gain + (w_up * above(hb, m, z) + w_down * under(hb, m, z))
+            share = inverse(total)
+            new = jnp.where(pinned, h, gain * share)
+            gb[m, z, PAD : PAD + yb, :] = new
+            wt[0, z] = w_x
+            wt[1, z] = w_high
+            wt[2, z] = w_up
+            wt[3, z] = w_down
+            wt[4, z] = share
+            return r_high, h, h_high, w_high, pack(2, m, z, new, packed)
+
+        r0, r1_ = layer(rb, m, 0), layer(rb, m, 1)
+        w_first = inverse(r0 + r1_)
+        start = (r1_, layer(hb, m, 0), layer(hb, m, 1), w_first, (zero, zero))
+        packed = lax.fori_loop(1, nz - 1, sweep, start, unroll=6)[-1]
+        send_edges(2, m, packed)
         g_edge = take_edges(2, gb, m)
 
-        @pl.loop(1, nz - 1)
-        def _(z):
-            h, h_sides = sides(gb, m, z, g_edge)
-            new = jnp.zeros_like(h)
-            for d in range(6):
-                new = new + wt[z, d] * h_sides[d]
-            ho[m, z] = jnp.where(pinned, h, new)
-
+        def again(z, carry):
+            h_low, h, w_low = carry
+            h_high = layer(gb, m, z + 1)
+            w_high = wt[1, z]
+            gain, _ = flow_x(wt[0, z], h, w_edge, g_edge, z)
+            gain = gain + (w_low * h_low + w_high * h_high)
+            gain = gain + (wt[2, z] * above(gb, m, z) + wt[3, z] * under(gb, m, z))
+            ho[m, z] = jnp.where(pinned, h, gain * wt[4, z])
+            return h, h_high, w_high
+
+        again_start = (layer(gb, m, 0), layer(gb, m, 1), w_first)
+        lax.fori_loop(1, nz - 1, again, again_start, unroll=10)
         pltpu.make_async_copy(ho.at[m], ho_hbm.at[m], out_sem.at[2 + m]).start()
 
     for m in members:
@@ -367,7 +403,7 @@
             pltpu.VMEM((2, nz, wide, xb), F32),
             pltpu.VMEM((2, nz, wide, xb), F32),
             pltpu.VMEM((2, nz, wide, xb), F32),
-            pltpu.VMEM((nz, 6, yb, xb), F32),
+            pltpu.VMEM((5, nz, yb, xb), F32),
             pltpu.VMEM((2, nz, yb, xb), F32),
             pltpu.VMEM((3, 2, 2, nz, xb), F32),
             pltpu.VMEM((3, 2, 2, nz, xb), F32),

time: 107 us -> 99.2 us (0.927)
  Pallas kernels: 102 us -> 93.8 us
    pallas_call x1, Pallas kernels: 102 us -> 93.8 us  [on_device(): pl.pallas_call(functools.partial(body, gx, gy, n, nz, yb, xb), out_shape=...]
where the time goes in v2:
time: 99.2 us; the launch traced here: 99 us
  Pallas kernels  93.8 us (95%)
  local copies, waits for them, and re-layouts  4.52 us (5%)
    pallas_call x1, Pallas kernels, on_device(): pl.pallas_call(functools.partial(body, gx, gy, n, nz, yb, xb), out_shape=...  93.8 us
    unnamed x2, local copies, waits for them, and re-layouts  4.52 us

profile of v2, /device:TPU:24, one launch (start us, length us, event | category | flops | bytes accessed | tf_op | source)
XLA Modules:
  0.0 99.0 jit_solution(6668057358964701639)
XLA Ops:
  0.6 93.8 %shard_map.59 = (f32[2,32,32,128]{3,2,1,0:T(8,128)}, f32[2,32,32,128]{3,2,1,0:T(8,128)}) custom-call(f32[2,32,32,128]{3,2,1,0:T(8,128)} %w_hbm.1, f32[2,32,32,128]{3,2,1,0:T(8,128)} %h_hbm.1, bf16[2,1024,1024]{2,1,0:T(8,128)(2,1)} %constant.4.clone.c_hbm, bf16[2,256,256]{2,1,0:T(8,128)(2,1)} %constant.5.clone.kz_hbm), custom_call_target="tpu_custom_call" | custom-call | flops 3221225472 | bytes 8388608 | tf_op jit(solution)/shard_map/pallas_call | solution.py:386
  94.5 2.3 %copy.8 = f32[2,32,32,128]{3,2,1,0:T(8,128)} copy(f32[2,32,32,128]{3,2,1,0:T(8,128)} %get-tuple-element.4) | data formatting | bytes 2097152
  96.7 2.3 %copy.9 = f32[2,32,32,128]{3,2,1,0:T(8,128)} copy(f32[2,32,32,128]{3,2,1,0:T(8,128)} %get-tuple-element.5) | data formatting | bytes 2097152

commit v3 on v2

--- a/solution.py
+++ b/solution.py
@@ -292,25 +292,26 @@
         h_left = jnp.where(first, e, pltpu.roll(h, 1, 1))
         return right * h_right + w_left * h_left, right + w_left
 
-    for m in members:
+    def resist(m):
         wait_all(lk.at[m], v3.at[m])
         pltpu.make_async_copy(lk.at[m], lk_hbm.at[m], out_sem.at[m]).start()
 
-        def resist(z, packed):
+        def step(z, packed):
             r = jnp.exp(-lk[m, z])
             rb[m, z, PAD : PAD + yb, :] = r
             return pack(1, m, z, r, packed)
 
-        send_edges(1, m, lax.fori_loop(0, nz, resist, (zero, zero), unroll=True))
+        send_edges(1, m, lax.fori_loop(0, nz, step, (zero, zero), unroll=True))
+        for z in (0, nz - 1):
+            gb[m, z, PAD : PAD + yb, :] = layer(hb, m, z)
+            ho[m, z] = layer(hb, m, z)
+
+    def first_sweep(m):
         h_edge = take_edges(0, hb, m)
         r_edge = take_edges(1, rb, m)
         w_edge = inverse(own_edges(1, m) + r_edge)
 
-        for z in (0, nz - 1):
-            gb[m, z, PAD : PAD + yb, :] = layer(hb, m, z)
-            ho[m, z] = layer(hb, m, z)
-
-        def sweep(z, carry):
+        def step(z, carry):
             r, h_low, h, w_low, packed = carry
             r_high = layer(rb, m, z + 1)
             h_high = layer(hb, m, z + 1)
@@ -325,33 +326,42 @@
             share = inverse(total)
             new = jnp.where(pinned, h, gain * share)
             gb[m, z, PAD : PAD + yb, :] = new
-            wt[0, z] = w_x
-            wt[1, z] = w_high
-            wt[2, z] = w_up
-            wt[3, z] = w_down
-            wt[4, z] = share
+            wt[m, 0, z] = w_x
+            wt[m, 1, z] = w_high
+            wt[m, 2, z] = w_up
+            wt[m, 3, z] = w_down
+            wt[m, 4, z] = share
             return r_high, h, h_high, w_high, pack(2, m, z, new, packed)
 
         r0, r1_ = layer(rb, m, 0), layer(rb, m, 1)
         w_first = inverse(r0 + r1_)
+        wt[m, 1, 0] = w_first
         start = (r1_, layer(hb, m, 0), layer(hb, m, 1), w_first, (zero, zero))
-        packed = lax.fori_loop(1, nz - 1, sweep, start, unroll=6)[-1]
-        send_edges(2, m, packed)
+        send_edges(2, m, lax.fori_loop(1, nz - 1, step, start, unroll=6)[-1])
+        return w_edge
+
+    def second_sweep(m, w_edge):
         g_edge = take_edges(2, gb, m)
 
-        def again(z, carry):
+        def step(z, carry):
             h_low, h, w_low = carry
             h_high = layer(gb, m, z + 1)
-            w_high = wt[1, z]
-            gain, _ = flow_x(wt[0, z], h, w_edge, g_edge, z)
+            w_high = wt[m, 1, z]
+            gain, _ = flow_x(wt[m, 0, z], h, w_edge, g_edge, z)
             gain = gain + (w_low * h_low + w_high * h_high)
-            gain = gain + (wt[2, z] * above(gb, m, z) + wt[3, z] * under(gb, m, z))
-            ho[m, z] = jnp.where(pinned, h, gain * wt[4, z])
+            gain = gain + (wt[m, 2, z] * above(gb, m, z) + wt[m, 3, z] * under(gb, m, z))
+            ho[m, z] = jnp.where(pinned, h, gain * wt[m, 4, z])
             return h, h_high, w_high
 
-        again_start = (layer(gb, m, 0), layer(gb, m, 1), w_first)
-        lax.fori_loop(1, nz - 1, again, again_start, unroll=10)
+        start = (layer(gb, m, 0), layer(gb, m, 1), wt[m, 1, 0])
+        lax.fori_loop(1, nz - 1, step, start, unroll=10)
         pltpu.make_async_copy(ho.at[m], ho_hbm.at[m], out_sem.at[2 + m]).start()
+
+    for m in members:
+        resist(m)
+    w_edges = [first_sweep(m) for m in members]
+    for m in members:
+        second_sweep(m, w_edges[m])
 
     for m in members:
         pltpu.make_async_copy(lk.at[m], lk_hbm.at[m], out_sem.at[m]).wait()
@@ -370,6 +380,18 @@
                 copy2(m, (i + k) % gx, s).wait_send()
 
         each3(m, lambda *at: None, lambda *at: copy3(*at).wait_send())
+
+
+def hand_over(lk_ref, ho_ref, lk_out, ho_out, sem):
+    copies = [
+        pltpu.make_async_copy(source.at[m], target.at[m], sem.at[2 * at + m])
+        for at, (source, target) in enumerate(((lk_ref, lk_out), (ho_ref, ho_out)))
+        for m in range(2)
+    ]
+    for copy in copies:
+        copy.start()
+    for copy in copies:
+        copy.wait()
 
 
 def on_device(gx, gy, white_noise, head_start):
@@ -383,9 +405,9 @@
     z_matrix = jnp.asarray(split_pair(np.kron(circulant(nz), np.eye(8))))
     block = jax.ShapeDtypeStruct(white_noise.shape, F32)
     dma = pltpu.SemaphoreType.DMA
-    return pl.pallas_call(
+    results = pl.pallas_call(
         functools.partial(body, gx, gy, n, nz, yb, xb),
-        out_shape=(block, block),
+        out_shape=(pltpu.VMEM(block.shape, F32),) * 2,
         in_specs=[pl.BlockSpec(memory_space=pl.ANY)] * 4,
         out_specs=(pl.BlockSpec(memory_space=pl.ANY),) * 2,
         scratch_shapes=[
@@ -403,7 +425,7 @@
             pltpu.VMEM((2, nz, wide, xb), F32),
             pltpu.VMEM((2, nz, wide, xb), F32),
             pltpu.VMEM((2, nz, wide, xb), F32),
-            pltpu.VMEM((5, nz, yb, xb), F32),
+            pltpu.VMEM((2, 5, nz, yb, xb), F32),
             pltpu.VMEM((2, nz, yb, xb), F32),
             pltpu.VMEM((3, 2, 2, nz, xb), F32),
             pltpu.VMEM((3, 2, 2, nz, xb), F32),
@@ -424,6 +446,13 @@
             flops=6 * 2 * rows * 2 * n * n, bytes_accessed=16 * n * xb * 4, transcendentals=2 * nz * yb * xb
         ),
     )(white_noise, head_start, matrix, z_matrix)
+    return pl.pallas_call(
+        hand_over,
+        out_shape=(block, block),
+        in_specs=[pl.BlockSpec(memory_space=pl.ANY)] * 2,
+        out_specs=(pl.BlockSpec(memory_space=pl.ANY),) * 2,
+        scratch_shapes=[dma((4,))],
+    )(*results)
 
 
 def solution(mesh):

time: 99.2 us -> 155 us (1.56)
  the two profiles are of different devices: /device:TPU:24 before, /device:TPU:1 now
where the time goes in v3:
time: 155 us
  Pallas kernels  153 us (99%)
  local copies, waits for them, and re-layouts  1.98 us (1%)
    pallas_call x1, Pallas kernels, on_device(): pl.pallas_call(functools.partial(body, gx, gy, n, nz, yb, xb), out_shape=...  87.8 us
    pallas_call x1, Pallas kernels, on_device(): pl.pallas_call(hand_over, out_shape=(block, block), in_specs=[pl.BlockSpe...  64.7 us

profile of v3, /device:TPU:1, one launch (start us, length us, event | category | flops | bytes accessed | tf_op | source)
XLA Modules:
  0.0 155.1 jit_solution(6039022462384291980)
XLA Ops:
  0.6 87.8 %shard_map.59 = (f32[2,32,32,128]{3,2,1,0:T(8,128)S(1)}, f32[2,32,32,128]{3,2,1,0:T(8,128)S(1)}) custom-call(f32[2,32,32,128]{3,2,1,0:T(8,128)} %w_hbm.1, f32[2,32,32,128]{3,2,1,0:T(8,128)} %h_hbm.1, bf16[2,1024,1024]{2,1,0:T(8,128)(2,1)} %constant.4.clone.c_hbm, bf16[2,256,256]{2,1,0:T(8,128)(2,1)} %constant.5.clone.kz_hbm), custom_call_target="tpu_custom_call" | custom-call | flops 3221225472 | bytes 8388608 | tf_op jit(solution)/shard_map/pallas_call | solution.py:408
  88.5 0.0 copy-start
  88.5 1.0 copy-done
  89.5 0.0 copy-start.1
  89.5 1.0 copy-done.1
  90.5 64.7 %shard_map.60 = (f32[2,32,32,128]{3,2,1,0:T(8,128)}, f32[2,32,32,128]{3,2,1,0:T(8,128)}) custom-call(f32[2,32,32,128]{3,2,1,0:T(8,128)} %copy-done, f32[2,32,32,128]{3,2,1,0:T(8,128)} %copy-done.1), custom_call_target="tpu_custom_call" | custom-call | tf_op jit(solution)/shard_map/pallas_call | solution.py:449
Async XLA Ops:
  88.5 1.0 copy-start
  89.5 1.0 copy-start.1

commit v4 on v3

--- a/solution.py
+++ b/solution.py
@@ -42,13 +42,20 @@
     return jnp.dot(a, b, preferred_element_type=F32)
 
 
-def blocks_of(gx, gy, i, j, s):
+def blocks_of(gx, gy, i, j, half):
     if (gx, gy) == (8, 32):
         core, z, y_lo = j % 2, (j // 2) % 8, j // 16
         x, y_hi = i % 4, i // 4
-        turn = (x + 2 * core * x) % 4
-        return (y_lo + y_hi) % 2 * 16 + (z + turn + 4 * s) % 8 * 2
-    return gy // gx * i + 2 * s
+        turn = x + 2 * core * x
+        return (y_lo + y_hi) % 2 * 16 + (z + turn) % 4 * 2 + 8 * half
+    return gy // gx * i + 2 * half
+
+
+def chunks_of(gx, gy, j, half):
+    if (gx, gy) == (8, 32):
+        y_lo = j // 16
+        return [((y_lo + y_hi) % 2 * 16 + 8 * half, range(4 * y_hi, 4 * y_hi + 4)) for y_hi in range(2)]
+    return [(0, range(gx))]
 
 
 def body(
@@ -61,7 +68,7 @@
     i = lax.axis_index("gx")
     j = lax.axis_index("gy")
     wide = yb + 2 * PAD
-    rows = 4 * yb
+    rows = 2 * yb
     members = range(2)
 
     w_in = [pltpu.make_async_copy(w_hbm.at[m], w_v.at[m], in_sem.at[m]) for m in members]
@@ -186,12 +193,12 @@
     def wait_all(ref, sem):
         pltpu.make_async_copy(ref, ref, sem).wait()
 
-    def copy2(m, to, s):
+    def copy2(m, half, to):
         return pltpu.make_async_remote_copy(
-            src_ref=yo.at[m, pl.ds(blocks_of(gx, gy, to, j, s), 2)],
-            dst_ref=r2.at[m, i, s],
-            send_sem=s2.at[m],
-            recv_sem=v2.at[m],
+            src_ref=yo.at[m, pl.ds(blocks_of(gx, gy, to, j, half), 2)],
+            dst_ref=r2.at[m, half, i],
+            send_sem=s2.at[m, half],
+            recv_sem=v2.at[m, half],
             device_id=(to, j),
             device_id_type=MESH,
         )
@@ -202,66 +209,68 @@
             high, low = split(r1[m, s])
             bcat[s * yb : (s + 1) * yb, 0:xb] = high
             bcat[s * yb : (s + 1) * yb, xb : 2 * xb] = low
-        for c in range(n // 256):
-            lines = slice(256 * c, 256 * (c + 1))
-            p = dot(c_v[0, lines, :], bcat[...])
-            r = p[:, :xb] + p[:, xb:] + dot(c_v[1, lines, :], bcat[:, 0:xb])
-            yo[m, per * c : per * (c + 1)] = r.reshape(per, yb, xb)
-        for s in range(2):
-            r2[m, i, s] = yo[m, pl.ds(blocks_of(gx, gy, i, j, s), 2)]
-
-        @pl.loop(1, gx)
-        def _(k):
-            for s in range(2):
-                copy2(m, (i + k) % gx, s).start()
-
-    def copy3(m, to, s, c):
+        for turn in range(2):
+            half = (j + turn) % 2
+            for start, takers in chunks_of(gx, gy, j, half):
+                lines = pl.ds(pl.multiple_of(start * yb, 256), 256)
+                p = dot(c_v[0, lines, :], bcat[...])
+                r = p[:, :xb] + p[:, xb:] + dot(c_v[1, lines, :], bcat[:, 0:xb])
+                yo[m, pl.ds(start, per)] = r.reshape(per, yb, xb)
+                for to in takers:
+
+                    @pl.when(to != i)
+                    def _():
+                        copy2(m, half, to).start()
+
+            r2[m, half, i] = yo[m, pl.ds(blocks_of(gx, gy, i, j, half), 2)]
+
+    def copy3(m, half, to, c):
         return pltpu.make_async_remote_copy(
-            src_ref=xo.at[m, to, s, c],
+            src_ref=xo.at[m, half, to, c],
             dst_ref=lk.at[m, j],
             send_sem=s3.at[m],
             recv_sem=v3.at[m],
-            device_id=(to, blocks_of(gx, gy, i, j, s) + c),
+            device_id=(to, blocks_of(gx, gy, i, j, half) + c),
             device_id_type=MESH,
         )
 
-    def each3(m, here, there):
-        @pl.loop(0, gx)
-        def _(k):
-            to = (i + k) % gx
-            for s in range(2):
-                for c in range(2):
-                    own = (to == i) & (blocks_of(gx, gy, i, j, s) + c == j)
-
-                    @pl.when(own)
-                    def _():
-                        here(m, to, s, c)
-
-                    @pl.when(jnp.logical_not(own))
-                    def _():
-                        there(m, to, s, c)
-
-    def keep3(m, to, s, c):
-        pltpu.make_async_copy(xo.at[m, to, s, c], lk.at[m, j], v3.at[m]).start()
+    def each3(m, half, to, here, there):
+        for c in range(2):
+            own = (to == i) & (blocks_of(gx, gy, i, j, half) + c == j)
+
+            @pl.when(own)
+            def _():
+                here(m, half, to, c)
+
+            @pl.when(jnp.logical_not(own))
+            def _():
+                there(m, half, to, c)
+
+    def keep3(m, half, to, c):
+        pltpu.make_async_copy(xo.at[m, half, to, c], lk.at[m, j], v3.at[m]).start()
 
     def filter_x(m):
-        for s in range(gx):
-            high, low = split(r2[m, s].reshape(rows, xb))
-            acat[0:rows, s * xb : (s + 1) * xb] = high
-            acat[rows : 2 * rows, s * xb : (s + 1) * xb] = low
-        for c in range(n // (2 * xb)):
-            cols = slice(2 * xb * c, 2 * xb * (c + 1))
-            p = dot(acat[...], c_v[0, :, cols])
-            r = p[:rows] + p[rows:] + dot(acat[0:rows, :], c_v[1, :, cols])
-            xo[m, 2 * c] = r[:, :xb].reshape(2, 2, yb, xb)
-            xo[m, 2 * c + 1] = r[:, xb:].reshape(2, 2, yb, xb)
-        each3(m, keep3, lambda *at: copy3(*at).start())
+        for turn in range(2):
+            half = (j + turn) % 2
+            wait_all(r2.at[m, half, pl.ds(0, gx - 1)], v2.at[m, half])
+            for s in range(gx):
+                high, low = split(r2[m, half, s].reshape(rows, xb))
+                acat[0:rows, s * xb : (s + 1) * xb] = high
+                acat[rows : 2 * rows, s * xb : (s + 1) * xb] = low
+            for turn_x in range(gx // 2):
+                pair = (i // 2 + turn_x) % (gx // 2)
+                cols = pl.ds(pl.multiple_of(pair * 2 * xb, 2 * xb), 2 * xb)
+                p = dot(acat[...], c_v[0, :, cols])
+                r = p[:rows] + p[rows:] + dot(acat[0:rows, :], c_v[1, :, cols])
+                for side in range(2):
+                    to = 2 * pair + side
+                    xo[m, half, to] = r[:, side * xb : (side + 1) * xb].reshape(2, yb, xb)
+                    each3(m, half, to, keep3, lambda *at: copy3(*at).start())
 
     c_in.wait()
     for m in members:
         wait_all(r1.at[m, pl.ds(0, gy - 1)], v1.at[m])
         filter_y(m)
-        wait_all(r2.at[m, pl.ds(0, gx - 1)], v2.at[m])
         filter_x(m)
 
     row_at = yb * j + lax.broadcasted_iota(jnp.int32, (yb, xb), 0)
@@ -374,24 +383,15 @@
         def _(k):
             copy1(m, k).wait_send()
 
-        @pl.loop(1, gx)
-        def _(k):
-            for s in range(2):
-                copy2(m, (i + k) % gx, s).wait_send()
-
-        each3(m, lambda *at: None, lambda *at: copy3(*at).wait_send())
-
-
-def hand_over(lk_ref, ho_ref, lk_out, ho_out, sem):
-    copies = [
-        pltpu.make_async_copy(source.at[m], target.at[m], sem.at[2 * at + m])
-        for at, (source, target) in enumerate(((lk_ref, lk_out), (ho_ref, ho_out)))
-        for m in range(2)
-    ]
-    for copy in copies:
-        copy.start()
-    for copy in copies:
-        copy.wait()
+        for half in range(2):
+
+            @pl.loop(1, gx)
+            def _(k):
+                copy2(m, half, (i + k) % gx).wait_send()
+
+            @pl.loop(0, gx)
+            def _(to):
+                each3(m, half, to, lambda *at: None, lambda *at: copy3(*at).wait_send())
 
 
 def on_device(gx, gy, white_noise, head_start):
@@ -399,7 +399,7 @@
     n = yb * gy
     assert n == xb * gx
     assert n == 4 * yb * gx and nz == gy
-    rows = 4 * yb
+    rows = 2 * yb
     wide = yb + 2 * PAD
     matrix = jnp.asarray(split_pair(circulant(n)))
     z_matrix = jnp.asarray(split_pair(np.kron(circulant(nz), np.eye(8))))
@@ -418,9 +418,9 @@
             pltpu.VMEM((2, gy, yb, xb), F32),
             pltpu.VMEM((n, 2 * xb), BF16),
             pltpu.VMEM((2, gy, yb, xb), F32),
-            pltpu.VMEM((2, gx, 2, 2, yb, xb), F32),
+            pltpu.VMEM((2, 2, gx, 2, yb, xb), F32),
             pltpu.VMEM((2 * rows, n), BF16),
-            pltpu.VMEM((2, gx, 2, 2, yb, xb), F32),
+            pltpu.VMEM((2, 2, gx, 2, yb, xb), F32),
             pltpu.VMEM((2, nz, yb, xb), F32),
             pltpu.VMEM((2, nz, wide, xb), F32),
             pltpu.VMEM((2, nz, wide, xb), F32),
@@ -434,7 +434,7 @@
             dma((4,)),
             dma((2,)),
             dma((2,)), dma((2,)),
-            dma((2,)), dma((2,)),
+            dma((2, 2)), dma((2, 2)),
             dma((2,)), dma((2,)),
             dma((3, 2, 4)), dma((3, 2, 4)),
             dma((4,)),
@@ -443,16 +443,10 @@
             collective_id=0, has_side_effects=True, vmem_limit_bytes=60 * 1024 * 1024
         ),
         cost_estimate=pl.CostEstimate(
-            flops=6 * 2 * rows * 2 * n * n, bytes_accessed=16 * n * xb * 4, transcendentals=2 * nz * yb * xb
+            flops=12 * 2 * rows * 2 * n * n, bytes_accessed=16 * n * xb * 4, transcendentals=2 * nz * yb * xb
         ),
     )(white_noise, head_start, matrix, z_matrix)
-    return pl.pallas_call(
-        hand_over,
-        out_shape=(block, block),
-        in_specs=[pl.BlockSpec(memory_space=pl.ANY)] * 2,
-        out_specs=(pl.BlockSpec(memory_space=pl.ANY),) * 2,
-        scratch_shapes=[dma((4,))],
-    )(*results)
+    return results
 
 
 def solution(mesh):

time: 155 us -> 86.7 us (0.56)
  Pallas kernels: 153 us -> 83.6 us
    pallas_call x1 -> x0, Pallas kernels: 64.7 us -> none  [on_device(): pl.pallas_call(hand_over, out_shape=(block, block), in_specs=[pl.BlockSpe...]
    pallas_call x1, Pallas kernels: 87.8 us -> 83.6 us  [on_device(): pl.pallas_call(functools.partial(body, gx, gy, n, nz, yb, xb), out_shape=...]
where the time goes in v4:
time: 86.7 us; the launch traced here: 86.2 us
  Pallas kernels  83.6 us (96%)
  local copies, waits for them, and re-layouts  1.94 us (2%)
    pallas_call x1, Pallas kernels, on_device(): pl.pallas_call(functools.partial(body, gx, gy, n, nz, yb, xb), out_shape=...  83.6 us
    unnamed x2, local copies, waits for them, and re-layouts  1.94 us

profile of v4, /device:TPU:1, one launch (start us, length us, event | category | flops | bytes accessed | tf_op | source)
XLA Modules:
  0.0 86.2 jit_solution(13820672109362217386)
XLA Ops:
  0.6 83.6 %shard_map.59 = (f32[2,32,32,128]{3,2,1,0:T(8,128)S(1)}, f32[2,32,32,128]{3,2,1,0:T(8,128)S(1)}) custom-call(f32[2,32,32,128]{3,2,1,0:T(8,128)} %w_hbm.1, f32[2,32,32,128]{3,2,1,0:T(8,128)} %h_hbm.1, bf16[2,1024,1024]{2,1,0:T(8,128)(2,1)} %constant.4.clone.c_hbm, bf16[2,256,256]{2,1,0:T(8,128)(2,1)} %constant.5.clone.kz_hbm), custom_call_target="tpu_custom_call" | custom-call | flops 3221225472 | bytes 8388608 | tf_op jit(solution)/shard_map/pallas_call | solution.py:408
  84.2 1.0 %copy.8 = f32[2,32,32,128]{3,2,1,0:T(8,128)} copy(f32[2,32,32,128]{3,2,1,0:T(8,128)S(1)} %get-tuple-element.2) | data formatting | bytes 2097152
  85.2 1.0 %copy.9 = f32[2,32,32,128]{3,2,1,0:T(8,128)} copy(f32[2,32,32,128]{3,2,1,0:T(8,128)S(1)} %get-tuple-element.3) | data formatting | bytes 2097152

commit v5 on v4

--- a/solution.py
+++ b/solution.py
@@ -62,7 +62,7 @@
     gx, gy, n, nz, yb, xb,
     w_hbm, h_hbm, c_hbm, kz_hbm, lk_hbm, ho_hbm,
     w_v, c_v, kz_v, zc, r1, bcat, yo, r2, acat, xo, lk,
-    hb, rb, gb, wt, ho, row_out, row_in, col_out, col_in,
+    hb, rb, gb, wt, ho, row_out, row_in, cols, col_in, corner_in,
     in_sem, c_sem, s1, v1, s2, v2, s3, v3, hs, hv, out_sem,
 ):
     i = lax.axis_index("gx")
@@ -97,6 +97,10 @@
     def _(k):
         pl.semaphore_signal(barrier, inc=1, device_id=(i, (j + k) % gy), device_id_type=MESH)
 
+    diagonal = [((i + (gx - 1, 1)[cs]) % gx, (j + (gy - 1, 1)[rs]) % gy) for cs in range(2) for rs in range(2)]
+    for peer in diagonal:
+        pl.semaphore_signal(barrier, inc=1, device_id=peer, device_id_type=MESH)
+
     def filter_z(m):
         for q in range(yb // 8):
             x = w_v[m, :, 8 * q : 8 * q + 8, :].reshape(nz * 8, xb)
@@ -125,7 +129,7 @@
     kz_in.wait()
     w_in[0].wait()
     filter_z(0)
-    pl.semaphore_wait(barrier, gx + gy - 2)
+    pl.semaphore_wait(barrier, gx + gy + 2)
     send1(0)
     w_in[1].wait()
     filter_z(1)
@@ -134,53 +138,75 @@
     lane = lax.broadcasted_iota(jnp.int32, (yb, xb), 1)
     first, last = lane == 0, lane == xb - 1
     even = lane % 2 == 0
-    peers = (
+    layer_0 = lane // 2
+    layer_1 = jnp.where(even, lane // 2 - 1, (lane + 1) % xb // 2)
+    around = (
         ((i + gx - 1) % gx, j),
         ((i + 1) % gx, j),
         (i, (j + gy - 1) % gy),
         (i, (j + 1) % gy),
+        *diagonal,
     )
 
-    def edge_copy(field, m, side):
-        out, inn = (col_out, col_in) if side < 2 else (row_out, row_in)
+    def edge_copy(field, m, at):
+        if at < 2:
+            source, target = cols.at[field, m], col_in.at[field, m, at]
+        elif at < 4:
+            source, target = row_out.at[field, m, at - 2], row_in.at[field, m, at - 2]
+        else:
+            start = (0, yb - 8)[at % 2]
+            source = cols.at[field, m, 0, pl.ds(start, 8)]
+            target = corner_in.at[field, m, at - 4]
         return pltpu.make_async_remote_copy(
-            src_ref=out.at[field, m, side % 2],
-            dst_ref=inn.at[field, m, side % 2],
-            send_sem=hs.at[field, m, side],
-            recv_sem=hv.at[field, m, side],
-            device_id=peers[side],
+            src_ref=source,
+            dst_ref=target,
+            send_sem=hs.at[field, m, at],
+            recv_sem=hv.at[field, m, at],
+            device_id=around[at],
             device_id_type=MESH,
         )
 
     zero = jnp.zeros((yb, xb), F32)
 
     def pack(field, m, z, x, packed):
-        to_left, to_right = packed
-        row_out[field, m, 0, pl.ds(z, 1), :] = x[0:1]
-        row_out[field, m, 1, pl.ds(z, 1), :] = x[yb - 1 : yb]
-        left_at = (2 * z + xb - 1) % xb
-        to_left = jnp.where(lane == left_at, pltpu.roll(x, left_at, 1), to_left)
-        to_right = jnp.where(lane == 2 * z, pltpu.roll(x, 2 * z + 1, 1), to_right)
-        return to_left, to_right
+        for side, at in enumerate((0, yb - 1)):
+            inner = (1, yb - 2)[side]
+            row_out[field, m, side, 0, pl.ds(z, 1), :] = x[at : at + 1]
+            row_out[field, m, side, 1, pl.ds(z, 1), :] = x[inner : inner + 1]
+        turned = pltpu.roll(x, 2 * z + 1, 1)
+        return (
+            jnp.where(layer_0 == z, turned, packed[0]),
+            jnp.where(layer_1 == z, turned, packed[1]),
+        )
 
     def send_edges(field, m, packed):
-        col_out[field, m, 0] = packed[0]
-        col_out[field, m, 1] = packed[1]
-        for side in range(4):
-            edge_copy(field, m, side).start()
+        cols[field, m, 0] = packed[0]
+        cols[field, m, 1] = packed[1]
+        for at in range(8):
+            edge_copy(field, m, at).start()
+
+    def to_left(x, by):
+        return pltpu.roll(x, x.shape[1] - by, 1)
 
     def take_edges(field, ref, m):
-        for side in range(4):
-            edge_copy(field, m, side).wait_recv()
-        for z in range(nz):
-            ref[m, z, PAD + yb : PAD + yb + 1, :] = row_in[field, m, 0, z : z + 1, :]
-            ref[m, z, PAD - 1 : PAD, :] = row_in[field, m, 1, z : z + 1, :]
-        return jnp.where(even, col_in[field, m, 1], col_in[field, m, 0])
-
-    def own_edges(field, m):
-        left = pltpu.roll(col_out[field, m, 0], 1, 1)
-        right = pltpu.roll(col_out[field, m, 1], xb - 1, 1)
-        return jnp.where(even, left, right)
+        for at in range(8):
+            edge_copy(field, m, at).wait_recv()
+        if ref is not None:
+            for z in range(nz):
+                ref[m, z, PAD + yb : PAD + yb + 1, :] = row_in[field, m, 0, 0, z : z + 1, :]
+                ref[m, z, PAD - 1 : PAD, :] = row_in[field, m, 1, 0, z : z + 1, :]
+        beside = jnp.where(even, col_in[field, m, 1, 0], to_left(col_in[field, m, 0, 0], 2))
+        beyond = jnp.where(
+            even, pltpu.roll(col_in[field, m, 1, 1], 1, 1), to_left(col_in[field, m, 0, 1], 3)
+        )
+        own = to_left(cols[field, m, 0], 1)
+        tile_even = even[0:8]
+
+        def corner(rs, at):
+            left, right = corner_in[field, m, 2 + rs], to_left(corner_in[field, m, rs], 2)
+            return jnp.where(tile_even, left, right)[at : at + 1]
+
+        return beside, beyond, own, corner(1, 7), corner(0, 0)
 
     for m in members:
         h_in[m].wait()
@@ -188,7 +214,7 @@
         def pack_head(z, packed):
             return pack(0, m, z, hb[m, z, PAD : PAD + yb, :], packed)
 
-        send_edges(0, m, lax.fori_loop(0, nz, pack_head, (zero, zero), unroll=16))
+        send_edges(0, m, lax.fori_loop(0, nz, pack_head, (zero, zero), unroll=True))
 
     def wait_all(ref, sem):
         pltpu.make_async_copy(ref, ref, sem).wait()
@@ -315,13 +341,67 @@
             gb[m, z, PAD : PAD + yb, :] = layer(hb, m, z)
             ho[m, z] = layer(hb, m, z)
 
-    def first_sweep(m):
-        h_edge = take_edges(0, hb, m)
-        r_edge = take_edges(1, rb, m)
-        w_edge = inverse(own_edges(1, m) + r_edge)
+    row_of = lax.broadcasted_iota(jnp.int32, (yb, xb), 0)
+    z_of = lax.broadcasted_iota(jnp.int32, (nz, xb), 0)
+    z_lane = lax.broadcasted_iota(jnp.int32, (nz, xb), 1)
+    z_col = xb * i + z_lane
+    row_pinned = (z_of == 0) | (z_of == nz - 1) | (z_col == 0) | (z_col == n - 1)
+    top = 2 * nz - 2
+    col_pinned = (row_at == 0) | (row_at == n - 1) | first | last | (lane == top) | (lane == top - 1)
+
+    def relaxed(r, h, pairs, kept):
+        weights = [inverse(r + r_beside) for r_beside, _ in pairs]
+        total = sum(weights[1:], weights[0])
+        gain = sum(w * h_beside for w, (_, h_beside) in zip(weights, pairs))
+        return jnp.where(kept, h, gain * inverse(total))
+
+    def ring(m, r_edges, h_edges):
+        def along_rows(edges, field, side):
+            beside, beyond = row_in[field, m, 1 - side, 0], row_in[field, m, 1 - side, 1]
+            corners = edges[3 + side]
+            pick = lambda at: jnp.sum(jnp.where(z_lane == at, corners, 0.0), axis=1, keepdims=True)
+            left, right = pick(2 * z_of), pick((2 * z_of + xb - 1) % xb)
+            return beside, (
+                beyond,
+                row_out[field, m, side, 0],
+                jnp.where(z_lane == 0, left, pltpu.roll(beside, 1, 1)),
+                jnp.where(z_lane == xb - 1, right, pltpu.roll(beside, xb - 1, 1)),
+                pltpu.roll(beside, 1, 0),
+                pltpu.roll(beside, nz - 1, 0),
+            )
+
+        for side in range(2):
+            r, r_pairs = along_rows(r_edges, 1, side)
+            h, h_pairs = along_rows(h_edges, 0, side)
+            new = relaxed(r, h, list(zip(r_pairs, h_pairs)), row_pinned)
+            at = (PAD - 1, PAD + yb)[side]
+            for z in range(nz):
+                gb[m, z, at : at + 1, :] = new[z : z + 1]
+
+        def along_cols(edges):
+            beside, beyond, own, up, down = edges
+            return beside, (
+                beyond,
+                own,
+                jnp.where(row_of == 0, up, pltpu.roll(beside, 1, 0)),
+                jnp.where(row_of == yb - 1, down, pltpu.roll(beside, yb - 1, 0)),
+                pltpu.roll(beside, 2, 1),
+                pltpu.roll(beside, xb - 2, 1),
+            )
+
+        r, r_pairs = along_cols(r_edges)
+        h, h_pairs = along_cols(h_edges)
+        return relaxed(r, h, list(zip(r_pairs, h_pairs)), col_pinned)
+
+    def sweeps(m):
+        h_edges = take_edges(0, hb, m)
+        r_edges = take_edges(1, rb, m)
+        h_edge = h_edges[0]
+        w_edge = inverse(r_edges[2] + r_edges[0])
+        g_edge = ring(m, r_edges, h_edges)
 
         def step(z, carry):
-            r, h_low, h, w_low, packed = carry
+            r, h_low, h, w_low = carry
             r_high = layer(rb, m, z + 1)
             h_high = layer(hb, m, z + 1)
             w_high = inverse(r + r_high)
@@ -333,51 +413,44 @@
             gain = gain + (w_low * h_low + w_high * h_high)
             gain = gain + (w_up * above(hb, m, z) + w_down * under(hb, m, z))
             share = inverse(total)
-            new = jnp.where(pinned, h, gain * share)
-            gb[m, z, PAD : PAD + yb, :] = new
-            wt[m, 0, z] = w_x
-            wt[m, 1, z] = w_high
-            wt[m, 2, z] = w_up
-            wt[m, 3, z] = w_down
-            wt[m, 4, z] = share
-            return r_high, h, h_high, w_high, pack(2, m, z, new, packed)
+            gb[m, z, PAD : PAD + yb, :] = jnp.where(pinned, h, gain * share)
+            wt[0, z] = w_x
+            wt[1, z] = w_high
+            wt[2, z] = w_up
+            wt[3, z] = w_down
+            wt[4, z] = share
+            return r_high, h, h_high, w_high
 
         r0, r1_ = layer(rb, m, 0), layer(rb, m, 1)
         w_first = inverse(r0 + r1_)
-        wt[m, 1, 0] = w_first
-        start = (r1_, layer(hb, m, 0), layer(hb, m, 1), w_first, (zero, zero))
-        send_edges(2, m, lax.fori_loop(1, nz - 1, step, start, unroll=6)[-1])
-        return w_edge
-
-    def second_sweep(m, w_edge):
-        g_edge = take_edges(2, gb, m)
-
-        def step(z, carry):
+        start = (r1_, layer(hb, m, 0), layer(hb, m, 1), w_first)
+        lax.fori_loop(1, nz - 1, step, start, unroll=6)
+
+        def again(z, carry):
             h_low, h, w_low = carry
             h_high = layer(gb, m, z + 1)
-            w_high = wt[m, 1, z]
-            gain, _ = flow_x(wt[m, 0, z], h, w_edge, g_edge, z)
+            w_high = wt[1, z]
+            gain, _ = flow_x(wt[0, z], h, w_edge, g_edge, z)
             gain = gain + (w_low * h_low + w_high * h_high)
-            gain = gain + (wt[m, 2, z] * above(gb, m, z) + wt[m, 3, z] * under(gb, m, z))
-            ho[m, z] = jnp.where(pinned, h, gain * wt[m, 4, z])
+            gain = gain + (wt[2, z] * above(gb, m, z) + wt[3, z] * under(gb, m, z))
+            ho[m, z] = jnp.where(pinned, h, gain * wt[4, z])
             return h, h_high, w_high
 
-        start = (layer(gb, m, 0), layer(gb, m, 1), wt[m, 1, 0])
-        lax.fori_loop(1, nz - 1, step, start, unroll=10)
+        start = (layer(gb, m, 0), layer(gb, m, 1), w_first)
+        lax.fori_loop(1, nz - 1, again, start, unroll=10)
         pltpu.make_async_copy(ho.at[m], ho_hbm.at[m], out_sem.at[2 + m]).start()
 
     for m in members:
         resist(m)
-    w_edges = [first_sweep(m) for m in members]
     for m in members:
-        second_sweep(m, w_edges[m])
+        sweeps(m)
 
     for m in members:
         pltpu.make_async_copy(lk.at[m], lk_hbm.at[m], out_sem.at[m]).wait()
         pltpu.make_async_copy(ho.at[m], ho_hbm.at[m], out_sem.at[2 + m]).wait()
-        for field in range(3):
-            for side in range(4):
-                edge_copy(field, m, side).wait_send()
+        for field in range(2):
+            for at in range(8):
+                edge_copy(field, m, at).wait_send()
 
         @pl.loop(1, gy)
         def _(k):
@@ -425,18 +498,19 @@
             pltpu.VMEM((2, nz, wide, xb), F32),
             pltpu.VMEM((2, nz, wide, xb), F32),
             pltpu.VMEM((2, nz, wide, xb), F32),
-            pltpu.VMEM((2, 5, nz, yb, xb), F32),
+            pltpu.VMEM((5, nz, yb, xb), F32),
             pltpu.VMEM((2, nz, yb, xb), F32),
-            pltpu.VMEM((3, 2, 2, nz, xb), F32),
-            pltpu.VMEM((3, 2, 2, nz, xb), F32),
-            pltpu.VMEM((3, 2, 2, yb, xb), F32),
-            pltpu.VMEM((3, 2, 2, yb, xb), F32),
+            pltpu.VMEM((2, 2, 2, 2, nz, xb), F32),
+            pltpu.VMEM((2, 2, 2, 2, nz, xb), F32),
+            pltpu.VMEM((2, 2, 2, yb, xb), F32),
+            pltpu.VMEM((2, 2, 2, 2, yb, xb), F32),
+            pltpu.VMEM((2, 2, 4, 8, xb), F32),
             dma((4,)),
             dma((2,)),
             dma((2,)), dma((2,)),
             dma((2, 2)), dma((2, 2)),
             dma((2,)), dma((2,)),
-            dma((3, 2, 4)), dma((3, 2, 4)),
+            dma((2, 2, 8)), dma((2, 2, 8)),
             dma((4,)),
         ],
         compiler_params=pltpu.CompilerParams(

time: 86.7 us -> 83.8 us (0.967)
  Pallas kernels: 83.6 us -> 80.8 us
    pallas_call x1, Pallas kernels: 83.6 us -> 80.8 us  [on_device(): pl.pallas_call(functools.partial(body, gx, gy, n, nz, yb, xb), out_shape=...]
where the time goes in v5:
time: 83.8 us; the launch traced here: 83.4 us
  Pallas kernels  80.8 us (96%)
  local copies, waits for them, and re-layouts  1.94 us (2%)
    pallas_call x1, Pallas kernels, on_device(): pl.pallas_call(functools.partial(body, gx, gy, n, nz, yb, xb), out_shape=...  80.8 us
    unnamed x2, local copies, waits for them, and re-layouts  1.94 us

profile of v5, /device:TPU:1, one launch (start us, length us, event | category | flops | bytes accessed | tf_op | source)
XLA Modules:
  0.0 83.4 jit_solution(17279328925992489880)
XLA Ops:
  0.6 80.8 %shard_map.59 = (f32[2,32,32,128]{3,2,1,0:T(8,128)S(1)}, f32[2,32,32,128]{3,2,1,0:T(8,128)S(1)}) custom-call(f32[2,32,32,128]{3,2,1,0:T(8,128)} %w_hbm.1, f32[2,32,32,128]{3,2,1,0:T(8,128)} %h_hbm.1, bf16[2,1024,1024]{2,1,0:T(8,128)(2,1)} %constant.4.clone.c_hbm, bf16[2,256,256]{2,1,0:T(8,128)(2,1)} %constant.5.clone.kz_hbm), custom_call_target="tpu_custom_call" | custom-call | flops 3221225472 | bytes 8388608 | tf_op jit(solution)/shard_map/pallas_call | solution.py:481
  81.4 1.0 %copy.8 = f32[2,32,32,128]{3,2,1,0:T(8,128)} copy(f32[2,32,32,128]{3,2,1,0:T(8,128)S(1)} %get-tuple-element.2) | data formatting | bytes 2097152
  82.4 1.0 %copy.9 = f32[2,32,32,128]{3,2,1,0:T(8,128)} copy(f32[2,32,32,128]{3,2,1,0:T(8,128)S(1)} %get-tuple-element.3) | data formatting | bytes 2097152

commit v6 on v5

--- a/solution.py
+++ b/solution.py
@@ -82,24 +82,25 @@
     c_in = pltpu.make_async_copy(c_hbm, c_v, c_sem.at[1])
     kz_in.start()
     w_in[0].start()
+
+    barrier = pltpu.get_barrier_semaphore()
+
+    @pl.loop(1, gx)
+    def _(k):
+        pl.semaphore_signal(barrier, inc=1, device_id=((i + k) % gx, j), device_id_type=MESH)
+
+    @pl.loop(1, gy)
+    def _(k):
+        pl.semaphore_signal(barrier, inc=1, device_id=(i, (j + k) % gy), device_id_type=MESH)
+
+    diagonal = [((i + (gx - 1, 1)[cs]) % gx, (j + (gy - 1, 1)[rs]) % gy) for cs in range(2) for rs in range(2)]
+    for peer in diagonal:
+        pl.semaphore_signal(barrier, inc=1, device_id=peer, device_id_type=MESH)
+
     w_in[1].start()
     h_in[0].start()
     h_in[1].start()
     c_in.start()
-
-    barrier = pltpu.get_barrier_semaphore()
-
-    @pl.loop(1, gx)
-    def _(k):
-        pl.semaphore_signal(barrier, inc=1, device_id=((i + k) % gx, j), device_id_type=MESH)
-
-    @pl.loop(1, gy)
-    def _(k):
-        pl.semaphore_signal(barrier, inc=1, device_id=(i, (j + k) % gy), device_id_type=MESH)
-
-    diagonal = [((i + (gx - 1, 1)[cs]) % gx, (j + (gy - 1, 1)[rs]) % gy) for cs in range(2) for rs in range(2)]
-    for peer in diagonal:
-        pl.semaphore_signal(barrier, inc=1, device_id=peer, device_id_type=MESH)
 
     def filter_z(m):
         for q in range(yb // 8):
@@ -133,6 +134,11 @@
     send1(0)
     w_in[1].wait()
     filter_z(1)
+
+    @pl.loop(1, gy)
+    def _(k):
+        copy1(0, k).wait_send()
+
     send1(1)
 
     lane = lax.broadcasted_iota(jnp.int32, (yb, xb), 1)
@@ -319,13 +325,11 @@
     def to_lane(packed, z):
         return pltpu.roll(packed, (xb - 2 * z) % xb, 1)
 
-    def flow_x(w, h, edge_w, edge_h, z):
-        right = jnp.where(last, to_lane(edge_w, z), w)
-        w_left = jnp.where(first, to_lane(edge_w, z), pltpu.roll(w, 1, 1))
-        e = to_lane(edge_h, z)
+    def flow_x(w_left, w_right, h, edge, z):
+        e = to_lane(edge, z)
         h_right = jnp.where(last, e, pltpu.roll(h, xb - 1, 1))
         h_left = jnp.where(first, e, pltpu.roll(h, 1, 1))
-        return right * h_right + w_left * h_left, right + w_left
+        return w_right * h_right + w_left * h_left
 
     def resist(m):
         wait_all(lk.at[m], v3.at[m])
@@ -408,13 +412,17 @@
             w_up = inverse(r + above(rb, m, z))
             w_down = inverse(r + under(rb, m, z))
             w_x = inverse(r + pltpu.roll(r, xb - 1, 1))
-            gain, total = flow_x(w_x, h, w_edge, h_edge, z)
-            total = total + ((w_low + w_high) + (w_up + w_down))
+            w_end = to_lane(w_edge, z)
+            w_left = jnp.where(first, w_end, pltpu.roll(w_x, 1, 1))
+            w_right = jnp.where(last, w_end, w_x)
+            gain = flow_x(w_left, w_right, h, h_edge, z)
+            total = (w_left + w_right) + ((w_low + w_high) + (w_up + w_down))
             gain = gain + (w_low * h_low + w_high * h_high)
             gain = gain + (w_up * above(hb, m, z) + w_down * under(hb, m, z))
             share = inverse(total)
             gb[m, z, PAD : PAD + yb, :] = jnp.where(pinned, h, gain * share)
-            wt[0, z] = w_x
+            wt[0, z] = w_left
+            wt[5, z] = w_right
             wt[1, z] = w_high
             wt[2, z] = w_up
             wt[3, z] = w_down
@@ -430,7 +438,7 @@
             h_low, h, w_low = carry
             h_high = layer(gb, m, z + 1)
             w_high = wt[1, z]
-            gain, _ = flow_x(wt[0, z], h, w_edge, g_edge, z)
+            gain = flow_x(wt[0, z], wt[5, z], h, g_edge, z)
             gain = gain + (w_low * h_low + w_high * h_high)
             gain = gain + (wt[2, z] * above(gb, m, z) + wt[3, z] * under(gb, m, z))
             ho[m, z] = jnp.where(pinned, h, gain * wt[4, z])
@@ -444,6 +452,10 @@
         resist(m)
     for m in members:
         sweeps(m)
+
+    @pl.loop(1, gy)
+    def _(k):
+        copy1(1, k).wait_send()
 
     for m in members:
         pltpu.make_async_copy(lk.at[m], lk_hbm.at[m], out_sem.at[m]).wait()
@@ -451,10 +463,6 @@
         for field in range(2):
             for at in range(8):
                 edge_copy(field, m, at).wait_send()
-
-        @pl.loop(1, gy)
-        def _(k):
-            copy1(m, k).wait_send()
 
         for half in range(2):
 
@@ -498,7 +506,7 @@
             pltpu.VMEM((2, nz, wide, xb), F32),
             pltpu.VMEM((2, nz, wide, xb), F32),
             pltpu.VMEM((2, nz, wide, xb), F32),
-            pltpu.VMEM((5, nz, yb, xb), F32),
+            pltpu.VMEM((6, nz, yb, xb), F32),
             pltpu.VMEM((2, nz, yb, xb), F32),
             pltpu.VMEM((2, 2, 2, 2, nz, xb), F32),
             pltpu.VMEM((2, 2, 2, 2, nz, xb), F32),

time: 83.8 us -> 82.6 us (0.986)
  Pallas kernels: 80.8 us -> 79 us
    pallas_call x1, Pallas kernels: 80.8 us -> 79 us  [on_device(): pl.pallas_call(functools.partial(body, gx, gy, n, nz, yb, xb), out_shape=...]
where the time goes in v6:
time: 82.6 us; the launch traced here: 81.6 us
  Pallas kernels  79 us (96%)
  local copies, waits for them, and re-layouts  1.94 us (2%)
    pallas_call x1, Pallas kernels, on_device(): pl.pallas_call(functools.partial(body, gx, gy, n, nz, yb, xb), out_shape=...  79 us
    unnamed x2, local copies, waits for them, and re-layouts  1.94 us

profile of v6, /device:TPU:1, one launch (start us, length us, event | category | flops | bytes accessed | tf_op | source)
XLA Modules:
  0.0 81.6 jit_solution(206073304726515154)
XLA Ops:
  0.6 79.0 %shard_map.59 = (f32[2,32,32,128]{3,2,1,0:T(8,128)S(1)}, f32[2,32,32,128]{3,2,1,0:T(8,128)S(1)}) custom-call(f32[2,32,32,128]{3,2,1,0:T(8,128)} %w_hbm.1, f32[2,32,32,128]{3,2,1,0:T(8,128)} %h_hbm.1, bf16[2,1024,1024]{2,1,0:T(8,128)(2,1)} %constant.4.clone.c_hbm, bf16[2,256,256]{2,1,0:T(8,128)(2,1)} %constant.5.clone.kz_hbm), custom_call_target="tpu_custom_call" | custom-call | flops 3221225472 | bytes 8388608 | tf_op jit(solution)/shard_map/pallas_call | solution.py:489
  79.6 1.0 %copy.8 = f32[2,32,32,128]{3,2,1,0:T(8,128)} copy(f32[2,32,32,128]{3,2,1,0:T(8,128)S(1)} %get-tuple-element.2) | data formatting | bytes 2097152
  80.6 1.0 %copy.9 = f32[2,32,32,128]{3,2,1,0:T(8,128)} copy(f32[2,32,32,128]{3,2,1,0:T(8,128)S(1)} %get-tuple-element.3) | data formatting | bytes 2097152

commit v7 on v6

--- a/solution.py
+++ b/solution.py
@@ -122,8 +122,8 @@
             device_id_type=MESH,
         )
 
-    def send1(m):
-        @pl.loop(1, gy)
+    def send1(m, start, end):
+        @pl.loop(start, end)
         def _(k):
             copy1(m, k).start()
 
@@ -131,15 +131,9 @@
     w_in[0].wait()
     filter_z(0)
     pl.semaphore_wait(barrier, gx + gy + 2)
-    send1(0)
+    send1(0, 1, gy)
     w_in[1].wait()
     filter_z(1)
-
-    @pl.loop(1, gy)
-    def _(k):
-        copy1(0, k).wait_send()
-
-    send1(1)
 
     lane = lax.broadcasted_iota(jnp.int32, (yb, xb), 1)
     first, last = lane == 0, lane == xb - 1
@@ -222,6 +216,12 @@
 
         send_edges(0, m, lax.fori_loop(0, nz, pack_head, (zero, zero), unroll=True))
 
+    @pl.loop(1, gy)
+    def _(k):
+        copy1(0, k).wait_send()
+
+    send1(1, 1, gy)
+
     def wait_all(ref, sem):
         pltpu.make_async_copy(ref, ref, sem).wait()
 
@@ -236,6 +236,7 @@
         )
 
     def filter_y(m):
+        wait_all(r1.at[m, pl.ds(0, gy - 1)], v1.at[m])
         per = 256 // yb
         for s in range(gy):
             high, low = split(r1[m, s])
@@ -281,8 +282,8 @@
     def keep3(m, half, to, c):
         pltpu.make_async_copy(xo.at[m, half, to, c], lk.at[m, j], v3.at[m]).start()
 
-    def filter_x(m):
-        for turn in range(2):
+    def filter_x(m, turns):
+        for turn in turns:
             half = (j + turn) % 2
             wait_all(r2.at[m, half, pl.ds(0, gx - 1)], v2.at[m, half])
             for s in range(gx):
@@ -300,10 +301,11 @@
                     each3(m, half, to, keep3, lambda *at: copy3(*at).start())
 
     c_in.wait()
-    for m in members:
-        wait_all(r1.at[m, pl.ds(0, gy - 1)], v1.at[m])
-        filter_y(m)
-        filter_x(m)
+    filter_y(0)
+    filter_x(0, (0,))
+    filter_y(1)
+    filter_x(0, (1,))
+    filter_x(1, (0, 1))
 
     row_at = yb * j + lax.broadcasted_iota(jnp.int32, (yb, xb), 0)
     col_at = xb * i + lane

time: 82.6 us -> 81.3 us (0.984); the launches traced: 81.6 us -> 81.2 us
  no operation moved by 1% of the time
where the time goes in v7:
time: 81.3 us; the launch traced here: 81.2 us
  Pallas kernels  78.6 us (97%)
  local copies, waits for them, and re-layouts  1.94 us (2%)
    pallas_call x1, Pallas kernels, on_device(): pl.pallas_call(functools.partial(body, gx, gy, n, nz, yb, xb), out_shape=...  78.6 us
    unnamed x2, local copies, waits for them, and re-layouts  1.94 us

profile of v7, /device:TPU:1, one launch (start us, length us, event | category | flops | bytes accessed | tf_op | source)
XLA Modules:
  0.0 81.2 jit_solution(10680319211410459780)
XLA Ops:
  0.6 78.6 %shard_map.59 = (f32[2,32,32,128]{3,2,1,0:T(8,128)S(1)}, f32[2,32,32,128]{3,2,1,0:T(8,128)S(1)}) custom-call(f32[2,32,32,128]{3,2,1,0:T(8,128)} %w_hbm.1, f32[2,32,32,128]{3,2,1,0:T(8,128)} %h_hbm.1, bf16[2,1024,1024]{2,1,0:T(8,128)(2,1)} %constant.4.clone.c_hbm, bf16[2,256,256]{2,1,0:T(8,128)(2,1)} %constant.5.clone.kz_hbm), custom_call_target="tpu_custom_call" | custom-call | flops 3221225472 | bytes 8388608 | tf_op jit(solution)/shard_map/pallas_call | solution.py:491
  79.2 1.0 %copy.8 = f32[2,32,32,128]{3,2,1,0:T(8,128)} copy(f32[2,32,32,128]{3,2,1,0:T(8,128)S(1)} %get-tuple-element.2) | data formatting | bytes 2097152
  80.2 1.0 %copy.9 = f32[2,32,32,128]{3,2,1,0:T(8,128)} copy(f32[2,32,32,128]{3,2,1,0:T(8,128)S(1)} %get-tuple-element.3) | data formatting | bytes 2097152
